TPU v7x, 32 devices: a whole 2x2x4 slice. The times are simulated.
32 devices in a mesh: wide: 8 (over z, y), narrow: 4 (over x, core).
Axes of the slice: x: 2, y: 2, z: 4, core: 2. Of those that a mesh axis runs over, the one named last changes fastest.
Arguments:
- prefit_resid: float32 [1310720], P(('wide', 'narrow')), may hold values from -6 to 6
- source_partials: float32 [5, 1310720], P(None, ('wide', 'narrow')), may hold values from -6 to 6
- attitude_partials: float32 [4, 1310720], P(None, ('wide', 'narrow')), may hold values from -0.25 to 0.25
- spline_position: float32 [1310720], P(('wide', 'narrow')), may hold values from 0 to 1
- calib_partials: float32 [3, 1310720], P(None, ('wide', 'narrow')), may hold values from -2 to 2
- obs_source: int32 [1310720], P(('wide', 'narrow')), may hold values from 0 to 127
- block_count: int32 [2048], P(('wide', 'narrow')), may hold values from 320 to 640, as said below
- obs_range: int32 [1310720], P(('wide', 'narrow')), may hold values from 0 to 7, as said below
- obs_knot: int32 [1310720], P(('wide', 'narrow')), may hold values from 0 to 255
- obs_unit: int32 [1310720], P(('wide', 'narrow')), may hold values from 0 to 2015
- given_inverse: float32 [8, 1024, 1024], P('wide'), may hold values from -2.5 to 2.5, as said below
- knot_decay: float32 [4, 2048], P(None, 'wide'), may hold values from 0.15 to 1
Outputs:
- source_update: float32 [5, 262144], P(None, ('wide', 'narrow'))
- attitude_update: float32 [4, 2048], P(None, 'wide')
- cal_update: float32 [3, 2016], P(None, 'narrow')
Inputs may be any that keep to these rules, and one draw needn't show every extreme that they name: `block_count`: each block's live observations are its first slots; every device has one block with all 640 slots live. `obs_range`: at most 10240 of one device's observation slots fall in one time range; for each index along narrow, some time range holds exactly 10240 slots of every device of that index. `given_inverse`: each time range's given inverse is symmetric.
All inputs are finite; a program needn't handle non-finite values.
Results may differ from a plain program's by a relative error of at most 0.0003.
Values sent between devices are 32-bit elements; how exact they have to be, the bound alone decides.
A program may use at most 64 MiB of HBM per device.

v0:
```python
import functools

import jax
import jax.numpy as jnp
from jax import lax
from jax.experimental import pallas as pl
from jax.experimental.pallas import tpu as pltpu
from jax.sharding import PartitionSpec as P

SRC_BLK = 128
SLOT_BLK = 640
CAL = 2016
SPLIT = 8
NT = (((1,), (1,)), ((), ()))
F32 = jnp.float32
BF16 = jnp.bfloat16


def source_row(i, j):
    d = i - j
    return d * 8 + i if d <= 4 else 3 * 8 + j


def ldl_solve(matrix, target):
    n = len(target)
    low = [[None] * n for _ in range(n)]
    inv = [None] * n
    for c in range(n):
        scaled = [low[c][b][1] for b in range(c)]
        d = matrix(c, c) + 1.0
        for b in range(c):
            d = d - scaled[b] * low[c][b][0]
        inv[c] = 1.0 / d
        for r in range(c + 1, n):
            v = matrix(r, c)
            for b in range(c):
                v = v - low[r][b][1] * low[c][b][0]
            low[r][c] = (v * inv[c], v)
    z = []
    for r in range(n):
        v = target[r]
        for b in range(r):
            v = v - low[r][b][0] * z[b]
        z.append(v)
    x = [None] * n
    for r in reversed(range(n)):
        v = z[r] * inv[r]
        for b in range(r + 1, n):
            v = v - low[b][r][0] * x[b]
        x[r] = v
    return x


def split3(v):
    hi = v.astype(BF16).astype(F32)
    rest = v - hi
    mid = rest.astype(BF16).astype(F32)
    return hi, mid, rest - mid


def source_kernel(
    blocks,
    count_ref, resid_hbm, sp_hbm, src_hbm,
    update_ref, after_ref,
    e_ref, s_ref, x_ref, iota_ref, resid_ref, sp_ref, src_ref, sems,
):
    moves = [(resid_hbm, resid_ref), (sp_hbm, sp_ref), (src_hbm, src_ref)]
    loads = [pltpu.make_async_copy(a, b, sems.at[k]) for k, (a, b) in enumerate(moves)]
    for load in loads:
        load.start()
    iota_ref[...] = lax.broadcasted_iota(jnp.int32, (SRC_BLK, 128), 0).astype(F32).astype(BF16)
    slot = lax.broadcasted_iota(jnp.int32, (1, SLOT_BLK), 1)
    for load in loads:
        load.wait()

    def normals(b, carry):
        at = pl.multiple_of(b * SLOT_BLK, 128)
        cols = pl.ds(at, SLOT_BLK)
        e = jnp.concatenate(
            [sp_ref[:, cols], resid_ref[:, cols], jnp.zeros((2, SLOT_BLK), F32)], axis=0
        )
        live = jnp.broadcast_to(slot < count_ref[b], (8, SLOT_BLK))
        e = jnp.where(live, e, 0.0)
        e_ref[:, cols] = e
        terms = jnp.concatenate(
            [e * e] + [e * pltpu.roll(e, d, axis=0) for d in range(1, 5)], axis=0
        )
        left = jnp.concatenate(split3(terms), axis=0).astype(BF16)
        src = src_ref[:, cols].astype(F32).astype(BF16)
        grid = jnp.concatenate([iota_ref[0:SRC_BLK, :]] * (SLOT_BLK // 128), axis=1)
        hot = jnp.where(grid == src, jnp.ones((), BF16), jnp.zeros((), BF16))
        sums = lax.dot_general(left, hot, NT, preferred_element_type=F32)
        s_ref[pl.ds(b, 40, stride=blocks), :] = sums[0:40] + sums[40:80] + sums[80:120]
        return carry

    lax.fori_loop(0, blocks, normals, 0, unroll=8)

    group = 16
    for g in range(0, blocks, group):
        def entry(i, j, g=g):
            row = source_row(i, j) * blocks + g
            return s_ref[row:row + group, :]

        x = ldl_solve(entry, [entry(5, j) for j in range(5)])
        for p in range(5):
            x_ref[pl.ds(g * 8 + p, group, stride=8), :] = x[p]
        x_ref[pl.ds(g * 8 + 5, group, stride=8), :] = jnp.full((group, 128), -1.0, F32)
        for p in (6, 7):
            x_ref[pl.ds(g * 8 + p, group, stride=8), :] = jnp.zeros((group, 128), F32)

    wide_slots = 2 * SLOT_BLK

    def residuals(t, carry):
        cols = pl.ds(pl.multiple_of(t * wide_slots, 128), wide_slots)
        src = src_ref[:, cols]
        gathered = []
        for half in range(2):
            b = t * 2 + half
            table = x_ref[pl.ds(pl.multiple_of(b * 8, 8), 8), :]
            update_ref[:, pl.ds(pl.multiple_of(b * 128, 128), 128)] = table[0:5, :]
            for q in range(SLOT_BLK // 128):
                lo = half * SLOT_BLK + q * 128
                ids = jnp.broadcast_to(src[:, lo:lo + 128], (8, 128))
                gathered.append(jnp.take_along_axis(table, ids, axis=1, mode="promise_in_bounds"))
        prod = e_ref[:, cols] * jnp.concatenate(gathered, axis=1)
        prod = prod + pltpu.roll(prod, 4, axis=0)
        prod = prod + pltpu.roll(prod, 2, axis=0)
        prod = prod + pltpu.roll(prod, 1, axis=0)
        after_ref[:, cols] = -prod[0:1, :]
        return carry

    lax.fori_loop(0, blocks // 2, residuals, 0, unroll=4)


def knots_kernel(
    blocks, wide, narrow,
    count_ref, after_hbm, att_hbm, pos_hbm, rng_hbm, knot_hbm, cal_hbm, unit_hbm, inverse_ref, decay_hbm,
    att_out, cal_out,
    after_ref, att_ref, pos_ref, rng_ref, knot_ref, cal_ref, unit_ref, g_ref, decay_ref,
    iota_ref, acc_att, acc_cal,
    send_att, recv_a, sum_a, recv_b, near_buf, recv_c, far_buf, recv_d,
    local_sem, send_n, got_n, send_w, got_w,
):
    w = lax.axis_index("wide")
    n = lax.axis_index("narrow")
    mesh_id = pl.DeviceIdType.MESH
    own = pl.ds(pl.multiple_of(n * 256, 256), 256)
    moves = [
        (after_hbm, after_ref), (att_hbm, att_ref), (pos_hbm, pos_ref), (rng_hbm, rng_ref),
        (knot_hbm, knot_ref), (cal_hbm, cal_ref), (unit_hbm, unit_ref),
        (inverse_ref.at[0, own], g_ref), (decay_hbm, decay_ref),
    ]
    loads = [pltpu.make_async_copy(a, b, local_sem.at[k]) for k, (a, b) in enumerate(moves)]
    for load in loads:
        load.start()

    barrier = pltpu.get_barrier_semaphore()
    narrow_to = [lax.rem(n + i, narrow) for i in range(narrow)]
    wide_to = [lax.rem(w + i, wide) for i in range(wide)]
    for i in range(1, narrow):
        pl.semaphore_signal(barrier, inc=1, device_id=(w, narrow_to[i]), device_id_type=mesh_id)
    for i in range(1, wide):
        pl.semaphore_signal(barrier, inc=1, device_id=(wide_to[i], n), device_id_type=mesh_id)

    sent = []

    class Step:
        def __init__(self, along_wide, at, source, slots):
            self.to = wide_to if along_wide else narrow_to
            self.me = w if along_wide else n
            self.out_sem = (send_w if along_wide else send_n).at[at]
            self.in_sem = (got_w if along_wide else got_n).at[at]
            self.along_wide, self.source, self.slots = along_wide, source, slots

        def copy(self, i, slot):
            d = self.to[i]
            return pltpu.make_async_remote_copy(
                src_ref=self.source(d), dst_ref=self.slots.at[slot],
                send_sem=self.out_sem.at[i], recv_sem=self.in_sem.at[slot],
                device_id=(d, n) if self.along_wide else (w, d), device_id_type=mesh_id,
            )

        def start(self):
            for i in range(1, len(self.to)):
                copy = self.copy(i, self.me)
                copy.start()
                sent.append(copy)

        def wait(self):
            for i in range(1, len(self.to)):
                self.copy(i, self.to[i]).wait_recv()

        def total(self):
            self.wait()
            value = self.slots[0]
            for k in range(1, len(self.to)):
                value = value + self.slots[k]
            return value

    iota_ref[...] = lax.broadcasted_iota(jnp.int32, (256, 128), 0).astype(F32).astype(BF16)
    acc_att[...] = jnp.zeros_like(acc_att)
    acc_cal[...] = jnp.zeros_like(acc_cal)
    wide_slots = 2 * SLOT_BLK
    sub8 = lax.broadcasted_iota(jnp.int32, (8, wide_slots), 0)
    first = sub8 < 4
    per = CAL // (narrow * SPLIT)
    per_row = 4 * per
    zero = jnp.zeros((), BF16)
    one = jnp.ones((), BF16)

    def horner(u, low, high):
        c = [jnp.where(first, low[i], high[i]) for i in range(4)]
        return c[0] + u * (c[1] + u * (c[2] + u * c[3]))

    def masked(ids, r, parts):
        here = ids == jnp.asarray(r, BF16)
        return [jnp.where(here, parts[k:k + 16], zero) for k in (0, 16)]

    def summed(acc, ids, count, pieces, place):
        ids = jnp.broadcast_to(ids.astype(F32).astype(BF16), (16, wide_slots))
        left = jnp.concatenate([v for r in range(count) for v in masked(ids, r, pieces)], axis=0)
        grid = jnp.concatenate([iota_ref[...]] * (wide_slots // 128), axis=1)
        hot = jnp.where(grid == place.astype(F32).astype(BF16), one, zero)
        acc[...] += lax.dot_general(left, hot, NT, preferred_element_type=F32)

    def attitude(t, carry):
        cols = pl.ds(pl.multiple_of(t * wide_slots, 128), wide_slots)
        after = jnp.broadcast_to(after_ref[:, cols], (8, wide_slots))
        u = jnp.broadcast_to(pos_ref[:, cols], (8, wide_slots))
        sixth = 1.0 / 6.0
        w01 = horner(u, (sixth, -0.5, 0.5, -sixth), (4.0 / 6.0, 0.0, -1.0, 0.5))
        w23 = horner(u, (sixth, 0.5, 0.5, -0.5), (0.0, 0.0, 0.0, sixth))
        att = att_ref[:, cols]
        scaled = jnp.concatenate([att, att], axis=0) * after
        terms = jnp.concatenate([scaled * w01, scaled * w23], axis=0)
        hi = terms.astype(BF16)
        pieces = jnp.concatenate([hi, (terms - hi.astype(F32)).astype(BF16)], axis=0)
        summed(acc_att, rng_ref[:, cols], wide, pieces, knot_ref[:, cols])
        return carry

    def calibration(t, carry):
        cols = pl.ds(pl.multiple_of(t * wide_slots, 128), wide_slots)
        slot = lax.broadcasted_iota(jnp.int32, (1, SLOT_BLK), 1)
        live = jnp.concatenate([slot < count_ref[2 * t], slot < count_ref[2 * t + 1]], axis=1)
        cal = jnp.where(live, cal_ref[:, cols], 0.0)
        four = jnp.concatenate([cal, after_ref[:, cols]], axis=0)
        f = jnp.concatenate([four, four], axis=0)
        near = f * jnp.where(first, f, pltpu.roll(f, 1, axis=0))
        far = f * pltpu.roll(f, 2, axis=0)
        far_hi, far_mid, far_lo = split3(far)
        far = jnp.where(sub8 < 2, far_hi, jnp.where(first, far_mid, jnp.where(sub8 < 6, far_lo, 0.0)))
        pieces = jnp.concatenate(list(split3(near)) + [far], axis=0).astype(BF16)
        unit = unit_ref[:, cols]
        upper = (unit * ((1 << 22) // per_row + 1)) >> 22
        place = unit - upper * per_row
        late = [jnp.where(place >= q * per, 64 - per, 0) for q in range(1, 4)]
        place = place + (late[0] + late[1] + late[2])
        summed(acc_cal, upper, narrow * 2, pieces, place)
        return carry

    def both(t, carry):
        return calibration(t, attitude(t, carry))

    for load in loads[0:7]:
        load.wait()
    lax.fori_loop(0, blocks // 2, both, 0, unroll=4)

    low = lax.broadcasted_iota(jnp.int32, (5, 128), 1) < 64
    units = []
    for pair in range(narrow * SPLIT // 2):
        top, half = pair // 2, (pair % 2) * 128
        part = acc_cal[top * 32:(top + 1) * 32, half:half + 128]
        near = part[0:8] + part[8:16] + part[16:24]
        far = part[24:26] + part[26:28] + part[28:30]
        upper5 = near[0:5]
        lower5 = jnp.concatenate([near[5:8], far], axis=0)
        units.append(jnp.where(low, upper5, pltpu.roll(lower5, 64, axis=1)))
        units.append(jnp.where(low, pltpu.roll(upper5, 64, axis=1), lower5))
    lane = lax.broadcasted_iota(jnp.int32, (4, 256), 1)
    before = None
    for r in range(wide):
        part = acc_att[r * 32:r * 32 + 16, :] + acc_att[r * 32 + 16:r * 32 + 32, :]
        rolled = [part[0:4]] + [pltpu.roll(part[4 * k:4 * k + 4], k, axis=1) for k in range(1, 4)]
        total = rolled[0]
        for k in range(1, 4):
            wrapped = jnp.zeros((4, 256), F32) if before is None else before[k]
            total = total + jnp.where(lane >= k, rolled[k], wrapped)
        before = rolled
        for k in range(narrow):
            send_att[k, r] = jnp.concatenate(
                [
                    total[k:k + 1, 0:128], total[k:k + 1, 128:256], units[k * SPLIT + r % SPLIT],
                    jnp.zeros((1, 128), F32),
                ],
                axis=0,
            )
    pl.semaphore_wait(barrier, narrow + wide - 2)
    step_a = Step(False, 0, lambda d: send_att.at[d], recv_a)
    step_a.start()
    recv_a[n] = send_att[n]
    sum_a[...] = step_a.total()
    step_b = Step(True, 0, lambda d: sum_a.at[d], recv_b)
    step_b.start()
    recv_b[w] = sum_a[w]

    total = step_b.total()
    for load in loads[7:]:
        load.wait()
    columns = total.T
    y = jnp.zeros((8, 1024), F32)
    for r in range(2):
        prod = columns[:, r:r + 1] * g_ref[r * 128:(r + 1) * 128, :]
        for j in range(16):
            y = y + prod[j * 8:(j + 1) * 8]
    y = jnp.sum(y, axis=0, keepdims=True)
    value = jnp.concatenate([y[:, c * 256:(c + 1) * 256] for c in range(4)], axis=0)
    mul = decay_ref[...]
    add = jnp.sqrt(1.0 - mul * mul) * value
    step = 1
    while step < 256:
        inside = lane >= step
        add = add + mul * jnp.where(inside, pltpu.roll(add, step, axis=1), 0.0)
        mul = mul * jnp.where(inside, pltpu.roll(mul, step, axis=1), 1.0)
        step *= 2
    near_buf[...] = jnp.concatenate([add[:, 0:128], add[:, 128:256]], axis=0)
    step_c = Step(False, 1, lambda d: near_buf, recv_c)
    step_c.start()
    recv_c[n] = near_buf[...]

    turned = pltpu.roll(total, 64, axis=1)
    q = [total[2 + j:3 + j] for j in range(5)] + [turned[2 + j:3 + j] for j in range(5)]
    pair = {(0, 0): q[0], (1, 1): q[1], (2, 2): q[2], (1, 0): q[5], (2, 1): q[6], (2, 0): q[8]}
    x = ldl_solve(lambda i, j: pair[(i, j)], [q[4], q[9], q[7]])
    x = pltpu.roll(jnp.concatenate(x + [jnp.zeros((5, 128), F32)], axis=0), 64, axis=1)

    whole = step_c.total()
    add = jnp.concatenate([whole[0:4], whole[4:8]], axis=1)
    last = jnp.concatenate(
        [jnp.broadcast_to(add[:, 255:256], (4, 128)), jnp.broadcast_to(mul[:, 255:256], (4, 128))],
        axis=0,
    )
    lane8 = lax.broadcasted_iota(jnp.int32, (8, 128), 1)
    far_buf[...] = jnp.where(lane8 < 64, last, x)
    step_d = Step(True, 1, lambda d: far_buf, recv_d)
    step_d.start()
    recv_d[w] = far_buf[...]

    step_d.wait()
    state = jnp.zeros((4, 128), F32)
    for p in range(wide):
        entry = recv_d[p]
        state = jnp.where(p < w, entry[4:8] * state + entry[0:4], state)
    att_out[...] = add + mul * jnp.broadcast_to(state[:, 0:1], (4, 256))

    base = (w // SPLIT) * SPLIT
    for j in range(SPLIT):
        cal_out[j] = recv_d[base + j]
    for copy in sent:
        copy.wait_send()


def finish_kernel(att_ref, cal_ref, att_out, cal_out):
    att_out[...] = att_ref[...]
    per = cal_out.shape[1] // SPLIT
    cal_out[...] = jnp.concatenate(
        [cal_ref[j, 0:3, 64:64 + per] for j in range(SPLIT)], axis=1
    )


def on_device(
    prefit_resid, source_partials, attitude_partials, spline_position, calib_partials, obs_source,
    block_count, obs_range, obs_knot, obs_unit, given_inverse, knot_decay,
):
    wide = lax.axis_size("wide")
    narrow = lax.axis_size("narrow")
    blocks = block_count.shape[0]
    slots = prefit_resid.shape[0]
    vmem = pl.BlockSpec(memory_space=pltpu.VMEM)
    hbm = pl.BlockSpec(memory_space=pltpu.HBM)
    row = lambda v: v.reshape(1, slots)
    limit = 56 * 1024 * 1024
    dma = pltpu.SemaphoreType.DMA
    ints = pltpu.VMEM((1, slots), jnp.int32)
    floats = pltpu.VMEM((1, slots), F32)
    source_update, after = pl.pallas_call(
        functools.partial(source_kernel, blocks),
        out_shape=(
            jax.ShapeDtypeStruct((5, blocks * SRC_BLK), F32),
            jax.ShapeDtypeStruct((1, slots), F32),
        ),
        in_specs=[pl.BlockSpec(memory_space=pltpu.SMEM)] + [hbm] * 3,
        out_specs=(vmem, vmem),
        scratch_shapes=[
            pltpu.VMEM((8, slots), F32),
            pltpu.VMEM((40 * blocks, 128), F32),
            pltpu.VMEM((8 * blocks, 128), F32),
            pltpu.VMEM((SRC_BLK, 128), BF16),
            floats,
            pltpu.VMEM((5, slots), F32),
            ints,
            dma((3,)),
        ],
        compiler_params=pltpu.CompilerParams(vmem_limit_bytes=limit),
        name="sources",
    )(block_count, row(prefit_resid), source_partials, row(obs_source))
    attitude_raw, cal = pl.pallas_call(
        functools.partial(knots_kernel, blocks, wide, narrow),
        out_shape=(
            jax.ShapeDtypeStruct(knot_decay.shape, F32),
            jax.ShapeDtypeStruct((SPLIT, 8, 128), F32),
        ),
        in_specs=[pl.BlockSpec(memory_space=pltpu.SMEM)] + [hbm] * 9,
        out_specs=(vmem, vmem),
        scratch_shapes=[
            floats,
            pltpu.VMEM((4, slots), F32),
            floats, ints, ints,
            pltpu.VMEM((3, slots), F32),
            ints,
            pltpu.VMEM((256, 1024), F32),
            pltpu.VMEM(knot_decay.shape, F32),
            pltpu.VMEM((256, 128), BF16),
            pltpu.VMEM((wide * 32, 256), F32),
            pltpu.VMEM((narrow * 2 * 32, 256), F32),
            pltpu.VMEM((narrow, wide, 8, 128), F32),
            pltpu.VMEM((narrow, wide, 8, 128), F32),
            pltpu.VMEM((wide, 8, 128), F32),
            pltpu.VMEM((wide, 8, 128), F32),
            pltpu.VMEM((8, 128), F32),
            pltpu.VMEM((narrow, 8, 128), F32),
            pltpu.VMEM((8, 128), F32),
            pltpu.VMEM((wide, 8, 128), F32),
            dma((9,)),
            dma((2, narrow)), dma((2, narrow)), dma((2, wide)), dma((2, wide)),
        ],
        compiler_params=pltpu.CompilerParams(
            collective_id=0, has_side_effects=True, vmem_limit_bytes=limit
        ),
        name="knots_units",
    )(
        block_count, after, attitude_partials, row(spline_position), row(obs_range), row(obs_knot),
        calib_partials, row(obs_unit), given_inverse, knot_decay,
    )
    attitude_update, cal_update = pl.pallas_call(
        finish_kernel,
        out_shape=(
            jax.ShapeDtypeStruct(knot_decay.shape, F32),
            jax.ShapeDtypeStruct((3, CAL // narrow), F32),
        ),
        in_specs=[vmem, vmem],
        out_specs=(vmem, vmem),
        compiler_params=pltpu.CompilerParams(vmem_limit_bytes=56 * 1024 * 1024),
        name="finish",
    )(attitude_raw, cal)
    return (source_update, attitude_update, cal_update)


def solution(mesh):
    both = P(("wide", "narrow"))
    rows = P(None, ("wide", "narrow"))
    placed = (
        both, rows, rows, both, rows, both, both, both, both, both, P("wide", None, None), P(None, "wide"),
    )
    return jax.shard_map(
        on_device,
        mesh=mesh,
        in_specs=placed,
        out_specs=(rows, P(None, "wide"), P(None, "narrow")),
        check_vma=False,
    )
```

profile of v0, /device:TPU:0, one launch (start us, length us, event | category | flops | bytes accessed | tf_op | source)
XLA Modules:
  0.0 44.4 jit_solution(1020725852126107413)
XLA Ops:
  0.6 9.8 %sources.1 = (f32[5,8192]{1,0:T(8,128)}, f32[1,40960]{1,0:T(1,128)}) custom-call(s32[64]{0:T(128)} %count_ref.3, f32[1,40960]{1,0:T(1,128)} %bitcast.10, f32[5,40960]{1,0:T(8,128)} %sp_hbm.1, s32[1,40960]{1,0:T(1,128)} %bitcast.11), custom_call_target="tpu_custom_call" | custom-call | tf_op jit(solution)/shard_map/sources/pallas_call | solution.py:385
  10.4 32.5 %knots_units.1 = (f32[4,256]{1,0:T(4,128)}, f32[8,8,128]{2,1,0:T(8,128)}) custom-call(s32[64]{0:T(128)} %count_ref.3, f32[1,40960]{1,0:T(1,128)} %get-tuple-element.10.after_hbm, f32[4,40960]{1,0:T(4,128)} %att_hbm.1, f32[1,40960]{1,0:T(1,128)} %bitcast.6, s32[1,40960]{1,0:T(1,128)} %bitcast.7, s32[1,40960]{1,0:T(1,128)} %bitcast.8, f32[3,40960]{1,0:T(4,128)} %cal_hbm.1, ...), custom_call_target="tpu_custom_call" | custom-call | tf_op jit(solution)/shard_map/knots_units/pallas_call | solution.py:406
  42.9 1.4 %finish.1 = (f32[4,256]{1,0:T(4,128)}, f32[3,504]{1,0:T(4,128)}) custom-call(f32[4,256]{1,0:T(4,128)} %get-tuple-element.11.att_ref, f32[8,8,128]{2,1,0:T(8,128)} %get-tuple-element.12.cal_ref), custom_call_target="tpu_custom_call" | custom-call | tf_op jit(solution)/shard_map/finish/pallas_call | solution.py:444
where the time goes:
time: 44.6 us; the launch traced here: 44.4 us
  Pallas kernels  43.7 us (98%)
  between operations  0.65 us (1%)
    pallas_call x1, Pallas kernels, on_device(): pl.pallas_call(functools.partial(knots_kernel, blocks, wide, narrow), out...  32.5 us
    pallas_call x1, Pallas kernels, on_device(): pl.pallas_call(functools.partial(source_kernel, blocks), out_shape=(jax.S...  9.75 us
    pallas_call x1, Pallas kernels, on_device(): pl.pallas_call(finish_kernel, out_shape=(jax.ShapeDtypeStruct(knot_decay....  1.44 us

commit v1 on v0

--- a/solution.py
+++ b/solution.py
@@ -93,7 +93,7 @@
         s_ref[pl.ds(b, 40, stride=blocks), :] = sums[0:40] + sums[40:80] + sums[80:120]
         return carry
 
-    lax.fori_loop(0, blocks, normals, 0, unroll=8)
+    lax.fori_loop(0, blocks, normals, 0, unroll=16)
 
     group = 16
     for g in range(0, blocks, group):
@@ -129,7 +129,7 @@
         after_ref[:, cols] = -prod[0:1, :]
         return carry
 
-    lax.fori_loop(0, blocks // 2, residuals, 0, unroll=4)
+    lax.fori_loop(0, blocks // 2, residuals, 0, unroll=8)
 
 
 def knots_kernel(
@@ -263,7 +263,7 @@
 
     for load in loads[0:7]:
         load.wait()
-    lax.fori_loop(0, blocks // 2, both, 0, unroll=4)
+    lax.fori_loop(0, blocks // 2, both, 0, unroll=8)
 
     low = lax.broadcasted_iota(jnp.int32, (5, 128), 1) < 64
     units = []

time: 44.6 us -> 42.8 us (0.960)
  Pallas kernels: 43.7 us -> 41.9 us
    pallas_call x1, Pallas kernels: 32.5 us -> 31.6 us  [on_device(): pl.pallas_call(functools.partial(knots_kernel, blocks, wide, narrow), out...]
    pallas_call x1, Pallas kernels: 9.75 us -> 8.87 us  [on_device(): pl.pallas_call(functools.partial(source_kernel, blocks), out_shape=(jax.S...]
where the time goes in v1:
time: 42.8 us; the launch traced here: 42.6 us
  Pallas kernels  41.9 us (98%)
  between operations  0.65 us (2%)
    pallas_call x1, Pallas kernels, on_device(): pl.pallas_call(functools.partial(knots_kernel, blocks, wide, narrow), out...  31.6 us
    pallas_call x1, Pallas kernels, on_device(): pl.pallas_call(functools.partial(source_kernel, blocks), out_shape=(jax.S...  8.87 us
    pallas_call x1, Pallas kernels, on_device(): pl.pallas_call(finish_kernel, out_shape=(jax.ShapeDtypeStruct(knot_decay....  1.44 us

profile of v1, /device:TPU:0, one launch (start us, length us, event | category | flops | bytes accessed | tf_op | source)
XLA Modules:
  0.0 42.6 jit_solution(11920111182610469767)
XLA Ops:
  0.6 8.9 %sources.1 = (f32[5,8192]{1,0:T(8,128)}, f32[1,40960]{1,0:T(1,128)}) custom-call(s32[64]{0:T(128)} %count_ref.3, f32[1,40960]{1,0:T(1,128)} %bitcast.10, f32[5,40960]{1,0:T(8,128)} %sp_hbm.1, s32[1,40960]{1,0:T(1,128)} %bitcast.11), custom_call_target="tpu_custom_call" | custom-call | tf_op jit(solution)/shard_map/sources/pallas_call | solution.py:385
  9.5 31.6 %knots_units.1 = (f32[4,256]{1,0:T(4,128)}, f32[8,8,128]{2,1,0:T(8,128)}) custom-call(s32[64]{0:T(128)} %count_ref.3, f32[1,40960]{1,0:T(1,128)} %get-tuple-element.10.after_hbm, f32[4,40960]{1,0:T(4,128)} %att_hbm.1, f32[1,40960]{1,0:T(1,128)} %bitcast.6, s32[1,40960]{1,0:T(1,128)} %bitcast.7, s32[1,40960]{1,0:T(1,128)} %bitcast.8, f32[3,40960]{1,0:T(4,128)} %cal_hbm.1, ...), custom_call_target="tpu_custom_call" | custom-call | tf_op jit(solution)/shard_map/knots_units/pallas_call | solution.py:406
  41.1 1.4 %finish.1 = (f32[4,256]{1,0:T(4,128)}, f32[3,504]{1,0:T(4,128)}) custom-call(f32[4,256]{1,0:T(4,128)} %get-tuple-element.11.att_ref, f32[8,8,128]{2,1,0:T(8,128)} %get-tuple-element.12.cal_ref), custom_call_target="tpu_custom_call" | custom-call | tf_op jit(solution)/shard_map/finish/pallas_call | solution.py:444
